TPU v7x, 768 devices: a whole 4x8x12 slice. The times are simulated.
768 devices in a mesh: group: 48 (over x, z), row: 8 (over y), col: 2 (over core).
Axes of the slice: x: 4, y: 8, z: 12, core: 2. Of those that a mesh axis runs over, the one named last changes fastest.
Arguments:
- activations: bfloat16 [12288, 8192], P('group', ('row', 'col')), may hold values from -6 to 6
- base_weight_codes: bfloat16 [8192, 8192], P('row', 'col'), may hold values from -6 to 6, as said below
- block_scale_exponents: int32 [256, 8192], P('row', 'col'), may hold values from -10 to -7
- adapter_down_weight: float32 [192, 8192, 64], P('group', ('row', 'col')), may hold values from -0.0625 to 0.0625
- adapter_up_weight: float32 [192, 64, 2, 8, 512], P('group', None, 'col', 'row'), may hold values from -0.75 to 0.75
- row_adapter_index: int32 [12288], P('group'), may hold values from 0 to 191, as said below
- adapter_storage_slot: int32 [192], replicated, may hold values from 0 to 191, as said below
Outputs:
- projected_layer_output: bfloat16 [12288, 2, 8, 512], P('group', 'col', 'row')
Inputs may be any that keep to these rules, and one draw needn't show every extreme that they name: `row_adapter_index`: every row of a group names an adapter; among the 256 rows of any one group, at most 12 name adapters whose slots lie in any one group's slots (slot // 4), and in every draw some group's slots receive exactly 12 rows from every group. A permutation: adapter a is stored in slot adapter_storage_slot[a], held by group adapter_storage_slot[a] // 4. `base_weight_codes`: each entry is one of the values 0, 0.5, 1, 1.5, 2, 3, 4, 6 or their negatives.
All inputs are finite; a program needn't handle non-finite values.
Results may differ from a plain program's by a relative error of at most 0.017.
Values may be sent and summed in bfloat16 or wider, within the bound.
A program may use at most 64 MiB of HBM per device.

v0:
```python
import jax
import jax.numpy as jnp
from jax import lax
from jax.sharding import PartitionSpec as P


def per_device(
    activations,
    base_weight_codes,
    block_scale_exponents,
    adapter_down_weight,
    adapter_up_weight,
    row_adapter_index,
    adapter_storage_slot,
):
    row_count = activations.shape[0]
    feature_block_index = activations.shape[1]
    inputs_here, outputs_here = base_weight_codes.shape
    scaling = jnp.exp2(block_scale_exponents.astype(jnp.float32)).astype(jnp.bfloat16)
    weight = (
        base_weight_codes.reshape(inputs_here // 32, 32, outputs_here) * scaling[:, None, :]
    ).reshape(inputs_here, outputs_here)
    row_blocks = lax.axis_size("row")
    block_width = outputs_here // row_blocks
    partial_out = jnp.dot(
        lax.all_gather(activations, "col", axis=1, tiled=True),
        weight,
        preferred_element_type=jnp.float32,
    )
    base_projection_output = lax.psum_scatter(
        partial_out.reshape(row_count, row_blocks, block_width).astype(jnp.bfloat16),
        "row",
        scatter_dimension=1,
        tiled=True,
    ).astype(jnp.float32)
    group_count = lax.axis_size("group")
    capacity = 9 * row_count // (4 * group_count)
    adapters_present = adapter_down_weight.shape[0]
    rank_feature_width = adapter_down_weight.shape[2]
    matches = (
        row_adapter_index[:, None]
        == jnp.arange(adapter_storage_slot.shape[0], dtype=jnp.int32)[None, :]
    )
    storage_slot_index = jnp.sum(jnp.where(matches, adapter_storage_slot[None, :], 0), axis=1)
    owner_group = storage_slot_index // adapters_present
    local_index = storage_slot_index % adapters_present
    owner_table = (
        owner_group[:, None] == jnp.arange(group_count, dtype=jnp.int32)[None, :]
    ).astype(jnp.int32)
    position = jnp.sum(owner_table * (jnp.cumsum(owner_table, axis=0) - 1), axis=1)
    target = owner_group * capacity + position
    chooser = target[None, :] == jnp.arange(group_count * capacity, dtype=jnp.int32)[:, None]
    chooser_bf = chooser.astype(jnp.bfloat16)
    send_rows = jnp.dot(chooser_bf, activations, preferred_element_type=jnp.float32).astype(
        jnp.bfloat16
    )
    send_rows = send_rows.reshape(group_count, capacity, feature_block_index)
    send_ids = jnp.max(jnp.where(chooser, local_index[None, :], -1), axis=1).reshape(
        group_count, capacity
    )
    down_weight_joined = jnp.transpose(adapter_down_weight, (1, 0, 2)).reshape(
        feature_block_index, adapters_present * rank_feature_width
    )
    up_weight_joined = adapter_up_weight.reshape(
        adapters_present * rank_feature_width, feature_block_index
    )
    rows_in = lax.all_to_all(send_rows, "group", split_axis=0, concat_axis=0, tiled=True)
    ids_in = lax.all_to_all(send_ids, "group", split_axis=0, concat_axis=0, tiled=True)
    source_rows, listed_entries = ids_in.shape
    flat_rows = rows_in.reshape(source_rows * listed_entries, feature_block_index).astype(
        jnp.float32
    )
    projected = jnp.dot(flat_rows, down_weight_joined, precision=lax.Precision.HIGHEST).reshape(
        source_rows * listed_entries, adapters_present, rank_feature_width
    )
    selector = (
        ids_in.reshape(-1)[:, None] == jnp.arange(adapters_present, dtype=jnp.int32)[None, :]
    ).astype(jnp.float32)[:, :, None]
    spread_part = (projected * selector).reshape(
        source_rows * listed_entries, adapters_present * rank_feature_width
    )
    spread_rows = lax.psum(spread_part, ("row", "col"))
    adapter_delta = jnp.dot(spread_rows, up_weight_joined, precision=lax.Precision.HIGHEST).astype(
        jnp.bfloat16
    )
    adapter_delta = adapter_delta.reshape(source_rows, listed_entries, feature_block_index)
    returned_value = lax.all_to_all(adapter_delta, "group", split_axis=0, concat_axis=0, tiled=True)
    delta_rows = jnp.dot(
        jnp.transpose(chooser_bf),
        returned_value.reshape(group_count * capacity, feature_block_index),
        preferred_element_type=jnp.float32,
    )
    projected_layer_output = (
        base_projection_output.reshape(row_count, feature_block_index) + delta_rows
    ).astype(jnp.bfloat16)
    return projected_layer_output.reshape(row_count, 1, 1, feature_block_index)


def solution(mesh):
    return jax.shard_map(
        per_device,
        mesh=mesh,
        in_specs=(
            P("group", ("row", "col")),
            P("row", "col"),
            P("row", "col"),
            P("group", ("row", "col"), None),
            P("group", None, "col", "row", None),
            P("group"),
            P(),
        ),
        out_specs=P("group", "col", "row", None),
        check_vma=False,
    )
```

profile of v0, /device:TPU:1, one launch (start us, length us, event | category | flops | bytes accessed | tf_op | source)
XLA Modules:
  0.0 255.7 jit_solution(17561361876275010124)
XLA Ops:
  7.4 0.0 copy-start
  7.4 0.9 select_reduce_fusion.1
  8.3 0.6 reduce-window.6
  8.9 0.2 slice_reduce_fusion
  9.1 0.1 fusion.6
  9.2 0.2 select_reduce_fusion
  9.4 0.7 all_to_all.13
  10.1 18.8 %all-to-all-start.1 = ((s32[48,1,12]{2,1,0:T(1,128)}), s32[48,1,12]{2,1,0:T(1,128)S(1)}, u32[]{:S(2)}, u32[]{:S(2)}) async-start(s32[48,1,12]{2,1,0:T(1,128)} %bitcast.10), calls=%async_computation.2 | async-start | bytes 49152 | tf_op jit(solution)/shard_map/all_to_all | solution.py:68
  29.0 1.3 convolution_convert_fusion.1
  30.3 1.1 reshape.143
  31.3 8.7 %all-to-all-done.1 = s32[48,1,12]{2,1,0:T(1,128)S(1)} async-done(((s32[48,1,12]{2,1,0:T(1,128)}), s32[48,1,12]{2,1,0:T(1,128)S(1)}, u32[]{:S(2)}, u32[]{:S(2)}) %all-to-all-start.1) | async-done | bytes 2336 | tf_op jit(solution)/shard_map/all_to_all | solution.py:68
  40.0 4.6 %all-to-all-start = ((bf16[48,12,512]{2,1,0:T(8,128)(2,1)}), bf16[48,12,512]{2,1,0:T(8,128)(2,1)S(1)}, u32[]{:S(2)}, u32[]{:S(2)}) async-start(bf16[48,12,512]{2,1,0:T(8,128)(2,1)} %reshape.143), calls=%async_computation.1 | async-start | bytes 1572864 | tf_op jit(solution)/shard_map/all_to_all | solution.py:67
  44.6 0.0 all-reduce.2.cloned.1.call-start
  44.6 1.1 exponential_convert_fusion
  45.8 0.0 copy-start.1
  45.8 7.3 %bitcast_multiply_fusion = bf16[1024,4096]{1,0:T(8,128)(2,1)} fusion(bf16[1024,4096]{1,0:T(8,128)(2,1)} %param.8, bf16[32,4096]{1,0:T(8,128)(2,1)S(1)} %exponential_convert_fusion), kind=kLoop, calls=%fused_computation | loop fusion | flops 4194304 | bytes 17039360 | tf_op jit(solution)/shard_map/mul | solution.py:21
  53.1 0.0 copy-done.1
  53.1 3.9 %all_gather.3 = bf16[256,1024]{1,0:T(8,128)(2,1)S(1)} all-gather(bf16[256,512]{1,0:T(8,128)(2,1)S(1)} %copy-done.1), channel_id=1, replica_groups=mesh['group'=48,'row'=8,'col'=2] {'col'}, dimensions={1}, use_global_device_ids=true | all-gather | bytes 786432 | tf_op jit(solution)/shard_map/all_gather | solution.py:26
  57.0 0.5 broadcast.172
  57.5 0.7 reduce.5
  58.2 0.1 eq.80
  58.4 14.7 %all-to-all-done = bf16[48,12,512]{2,1,0:T(8,128)(2,1)S(1)} async-done(((bf16[48,12,512]{2,1,0:T(8,128)(2,1)}), bf16[48,12,512]{2,1,0:T(8,128)(2,1)S(1)}, u32[]{:S(2)}, u32[]{:S(2)}) %all-to-all-start) | async-done | bytes 589856 | tf_op jit(solution)/shard_map/all_to_all | solution.py:67
  73.0 0.1 reshape.153
  73.2 0.0 copy-done
  73.2 1.7 convolution_multiply_fusion
  74.9 0.0 all-reduce.2.cloned.1.call-update
  74.9 0.0 reduce-scatter.2.cloned.1.call-start
  75.0 5.9 %convolution_convert_fusion = bf16[4096,256]{1,0:T(8,128)(2,1)S(1)} fusion(bf16[1024,4096]{1,0:T(8,128)(2,1)} %bitcast_multiply_fusion, bf16[256,1024]{1,0:T(8,128)(2,1)S(1)} %all_gather.3), kind=kOutput, calls=%fused_computation.1 | convolution fusion | flops 2148532224 | bytes 11010048 | tf_op jit(solution)/shard_map/dot_general | solution.py:25
  80.9 2.4 copy.14
  83.3 0.0 reduce-scatter.2.cloned.1.call-update
  83.3 1.1 copy.17
  84.4 117.0 %all-reduce.2.cloned.1.call-done = f32[576,256]{0,1:T(8,128)} async-done(((f32[576,256]{0,1:T(8,128)}), f32[576,256]{0,1:T(8,128)}) %all-reduce.2.cloned.1.call-update) | async-done | bytes 589840 | tf_op jit(solution)/shard_map/psum | solution.py:82
  201.4 2.4 convolution_convert_fusion.2
  203.8 0.1 reshape.148
  203.9 42.1 %all_to_all.19 = bf16[48,12,512]{2,1,0:T(8,128)(2,1)S(1)} all-to-all(bf16[48,12,512]{2,1,0:T(8,128)(2,1)S(1)} %reshape.148), channel_id=1, replica_groups=mesh['group'=48,'row'=8,'col'=2] {'group'}, dimensions={0} | all-to-all | bytes 1179648 | tf_op jit(solution)/shard_map/all_to_all | solution.py:87
  246.0 0.1 reshape.149
  246.1 0.0 reduce-scatter.2.cloned.1.call-done
  246.2 2.1 fusion.1
  (7 shorter events, 0.1 us)
Async XLA Ops:
  7.4 65.8 %copy-start = (f32[4,512,64]{1,2,0:T(8,128)S(1)}, f32[4,512,64]{1,2,0:T(8,128)}, u32[]{:S(2)}) copy-start(f32[4,512,64]{1,2,0:T(8,128)} %param.10) | copy-start | bytes 1572868
  10.1 29.9 %all-to-all-start.1 = ((s32[48,1,12]{2,1,0:T(1,128)}), s32[48,1,12]{2,1,0:T(1,128)S(1)}, u32[]{:S(2)}, u32[]{:S(2)}) async-start(s32[48,1,12]{2,1,0:T(1,128)} %bitcast.10), calls=%async_computation.2 | async-start | bytes 49152 | tf_op jit(solution)/shard_map/all_to_all | solution.py:68
  40.0 33.0 %all-to-all-start = ((bf16[48,12,512]{2,1,0:T(8,128)(2,1)}), bf16[48,12,512]{2,1,0:T(8,128)(2,1)S(1)}, u32[]{:S(2)}, u32[]{:S(2)}) async-start(bf16[48,12,512]{2,1,0:T(8,128)(2,1)} %reshape.143), calls=%async_computation.1 | async-start | bytes 1572864 | tf_op jit(solution)/shard_map/all_to_all | solution.py:67
  44.6 156.8 %all-reduce.2.cloned.1.call-start = ((), (), s32[]{:S(2)}) async-start(), calls=%async_computation.5 | async-start | bytes 1310720 | tf_op jit(solution)/shard_map/psum | solution.py:82
  45.8 7.4 %copy-start.1 = (bf16[256,512]{1,0:T(8,128)(2,1)S(1)}, bf16[256,512]{1,0:T(8,128)(2,1)}, u32[]{:S(2)}) copy-start(bf16[256,512]{1,0:T(8,128)(2,1)} %param.7) | copy-start | bytes 786436
  74.9 171.2 %reduce-scatter.2.cloned.1.call-start = ((), (), s32[]{:S(2)}) async-start(), calls=%async_computation.4 | async-start | bytes 2359296 | tf_op jit(solution)/shard_map/reduce_scatter | solution.py:30
Sparse Core Ops, SparseCore 0:
  75.1 126.2 all-reduce.1
Sparse Core Ops, SparseCore 1:
  83.4 43.0 reduce-scatter.1
where the time goes:
time: 261 us; the launch traced here: 256 us
  waiting for transfers between devices  140 us (54%)
  blocking collectives  46 us (18%)
  starting transfers between devices  23.5 us (9%)
  between operations  15 us (6%)
  matrix products  13.4 us (5%)
  other arithmetic  11 us (4%)
  local copies, waits for them, and re-layouts  6.46 us (2%)
    psum x1, waiting for transfers between devices, per_device(): spread_rows = lax.psum(spread_part, ('row', 'col'))  117 us
    all_to_all x1, blocking collectives, per_device(): lax.all_to_all(adapter_delta, 'group', split_axis=0, concat_axis=0, tiled...  42.1 us
    all_to_all x1, starting transfers between devices, per_device(): lax.all_to_all(send_ids, 'group', split_axis=0, concat_axis=0, tiled=True)  18.8 us
    all_to_all x1, waiting for transfers between devices, per_device(): lax.all_to_all(send_rows, 'group', split_axis=0, concat_axis=0, tiled=True)  14.7 us
    all_to_all x1, waiting for transfers between devices, per_device(): lax.all_to_all(send_ids, 'group', split_axis=0, concat_axis=0, tiled=True)  8.69 us
    mul x1, other arithmetic, per_device(): base_weight_codes.reshape(inputs_here // 32, 32, outputs_here)  7.34 us
    dot_general x1, matrix products, per_device(): jnp.dot(lax.all_gather(activations, 'col', axis=1, tiled=True), weight, p...  5.89 us
  transfers between devices with their start and end apart: 4, of which 3 were waited for; matrix products, arithmetic and copies ran while one was open for 9% of the time, Pallas kernels for 0%

commit v1 on v0

v1 whole, which is shorter than its diff:
```python
import functools

import jax
import jax.numpy as jnp
from jax import lax
from jax.experimental import pallas as pl
from jax.experimental.pallas import tpu as pltpu
from jax.sharding import PartitionSpec as P

MESH = pl.DeviceIdType.MESH
F32 = jnp.float32
BF16 = jnp.bfloat16
I32 = jnp.int32

NX = 4
NZ = 12
NROW = 8
NFLAT = 16
ROWS = 256
FEAT = 512
BLK = 48
RANK = 64
AD = 4
SLAB_W = NX * AD * RANK

ORDER = (0, 1, 11, 2, 10, 3, 9, 4, 8, 5, 7, 6)
CHUNKS = ((0, 12),)


def kernel(
    act_h,
    codes_h,
    scl_h,
    down_h,
    up_h,
    ids_ref,
    tab_ref,
    out_ref,
    a_all,
    w_v,
    scl_v,
    down_v,
    up_v,
    tab_v,
    choose,
    xs,
    xr,
    ids_s,
    ids_r,
    d_all,
    u_all,
    part,
    sp,
    sm,
    rp,
    rm,
    low_s,
    red,
    low_full,
    back_s,
    back_r,
    acc,
    load_sem,
    w_sem,
    a_sem,
    x_send,
    x_recv,
    i_send,
    i_recv,
    ad_send,
    ad_recv,
    rs_send,
    rs_recv,
    low_send,
    red_recv,
    full_send,
    full_recv,
    b_send,
    b_recv,
):
    g = lax.axis_index("group")
    r = lax.axis_index("row")
    c = lax.axis_index("col")
    x = g // NZ
    z = g % NZ
    flat = 2 * r + c

    def at_z(offset):
        return (x * NZ + (z + offset + NZ) % NZ, r, c)

    def at_x(offset):
        return (((x + offset + NX) % NX) * NZ + z, r, c)

    def at_row(offset):
        return (g, (r + offset + NROW) % NROW, c)

    def block_of(i):
        return (r + 4 + ((i + 1) // 2) * (1 - 2 * (i % 2)) + NROW) % NROW

    load_a = pltpu.make_async_copy(act_h, a_all.at[c], load_sem.at[0])
    load_s = pltpu.make_async_copy(scl_h, scl_v, load_sem.at[1])
    load_d = pltpu.make_async_copy(down_h, down_v, load_sem.at[2])
    load_u = pltpu.make_async_copy(up_h, up_v, load_sem.at[3])

    def load_w(i):
        columns = pl.ds(pl.multiple_of(block_of(i) * FEAT, FEAT), FEAT)
        return pltpu.make_async_copy(codes_h.at[:, columns], w_v.at[i], w_sem.at[i])

    load_a.start()
    load_w(0).start()
    load_s.start()
    load_d.start()
    for i in range(1, NROW):
        load_w(i).start()
    load_u.start()

    barrier = pltpu.get_barrier_semaphore()
    peers = [at_z(o) for o in range(1, NZ)]
    peers += [at_x(o) for o in range(1, NX)]
    for device in peers:
        pl.semaphore_signal(barrier, inc=1, device_id=device, device_id_type=MESH)

    def greet(i, carry):
        pl.semaphore_signal(
            barrier,
            inc=1,
            device_id=(g, (r + i // 2) % NROW, (c + i % 2) % 2),
            device_id_type=MESH,
        )
        return carry

    lax.fori_loop(1, NFLAT, greet, 0)

    tab_v[...] = jnp.zeros(tab_v.shape, F32)
    tab_v[:, : tab_ref.shape[1]] = tab_ref[...].astype(F32)
    ids = ids_ref[...]
    match = (lax.broadcasted_iota(I32, (256, ROWS), 0) == ids).astype(F32).astype(BF16)
    slots = jnp.dot(
        jnp.broadcast_to(tab_v[...], (8, 256)).astype(BF16), match, preferred_element_type=F32
    ).astype(I32)
    owner = slots >> 2
    owner_x = (
        (owner >= NZ).astype(I32) + (owner >= 2 * NZ).astype(I32) + (owner >= 3 * NZ).astype(I32)
    )
    away = z - (owner - NZ * owner_x)
    away = jnp.where(away < 0, away + NZ, away)
    place = jnp.zeros_like(away)
    for q, o in enumerate(ORDER):
        place = jnp.where(away == o, q, place)
    adapter = (owner_x * AD + (slots & 3) + 1).astype(F32).astype(BF16)
    sent_to = lax.broadcasted_iota(I32, (16, ROWS), 0) == place[0:1]
    before = (
        lax.broadcasted_iota(I32, (ROWS, ROWS), 0) < lax.broadcasted_iota(I32, (ROWS, ROWS), 1)
    )
    prefix = jnp.dot(
        sent_to.astype(F32).astype(BF16),
        before.astype(F32).astype(BF16),
        preferred_element_type=F32,
    )
    position = jnp.sum(jnp.where(sent_to, prefix, 0.0), axis=0, keepdims=True).astype(I32)
    target = place[0:1] * BLK + position
    choose[...] = (
        (lax.broadcasted_iota(I32, (NZ * BLK, ROWS), 0) == target).astype(F32).astype(BF16)
    )
    ids_s[...] = jnp.zeros(ids_s.shape, F32)
    for q in range(NZ):
        row = lax.dot_general(
            adapter,
            choose[q * BLK : (q + 1) * BLK, :],
            (((1,), (1,)), ((), ())),
            preferred_element_type=F32,
        )
        ids_s[q, :, 0:BLK] = row[0:1]
    ids_r[0] = ids_s[0]
    load_a.wait()
    xs[...] = jnp.dot(choose[...], a_all[c], preferred_element_type=F32).astype(BF16)
    xr[0:BLK] = xs[0:BLK]

    pl.semaphore_wait(barrier, len(peers) + NFLAT - 1)

    def send_rows(q):
        rows = pl.ds(q * BLK, BLK)
        return pltpu.make_async_remote_copy(
            src_ref=xs.at[rows],
            dst_ref=xr.at[rows],
            send_sem=x_send.at[q],
            recv_sem=x_recv.at[q],
            device_id=at_z(-ORDER[q]),
            device_id_type=MESH,
        )

    def send_ids(q):
        return pltpu.make_async_remote_copy(
            src_ref=ids_s.at[q],
            dst_ref=ids_r.at[q],
            send_sem=i_send.at[q],
            recv_sem=i_recv.at[q],
            device_id=at_z(-ORDER[q]),
            device_id_type=MESH,
        )

    def send_back(q):
        rows = pl.ds(q * BLK, BLK)
        return pltpu.make_async_remote_copy(
            src_ref=back_s.at[rows],
            dst_ref=back_r.at[rows],
            send_sem=b_send.at[q],
            recv_sem=b_recv.at[q],
            device_id=at_z(ORDER[q]),
            device_id_type=MESH,
        )

    swap_a = pltpu.make_async_remote_copy(
        src_ref=a_all.at[c],
        dst_ref=a_all.at[c],
        send_sem=a_sem.at[0],
        recv_sem=a_sem.at[1],
        device_id=(g, r, 1 - c),
        device_id_type=MESH,
    )
    take_a = pltpu.make_async_remote_copy(
        src_ref=a_all.at[1 - c],
        dst_ref=a_all.at[1 - c],
        send_sem=a_sem.at[0],
        recv_sem=a_sem.at[1],
        device_id=(g, r, 1 - c),
        device_id_type=MESH,
    )
    swap_a.start()
    for q in range(1, NZ):
        send_ids(q).start()
        send_rows(q).start()

    def share(buffer, base, kind):
        half = AD * RANK // 2
        where = {
            "right": (x, pl.ds(0, 2 * half), 1),
            "left": (x, pl.ds(0, 2 * half), -1),
            "far_right": ((x + NX - 1) % NX, pl.ds(0, half), 1),
            "far_left": ((x + 1) % NX, pl.ds(half, half), -1),
        }
        at, rows, step = where[kind]
        n = base + ("right", "left", "far_right", "far_left").index(kind)
        return pltpu.make_async_remote_copy(
            src_ref=buffer.at[at, rows],
            dst_ref=buffer.at[at, rows],
            send_sem=ad_send.at[n],
            recv_sem=ad_recv.at[n],
            device_id=at_x(step),
            device_id_type=MESH,
        )

    def arrived(buffer, base, kind):
        half = AD * RANK // 2
        where = {
            "right": ((x + NX - 1) % NX, pl.ds(0, 2 * half)),
            "left": ((x + 1) % NX, pl.ds(0, 2 * half)),
            "far_right": ((x + 2) % NX, pl.ds(0, half)),
            "far_left": ((x + 2) % NX, pl.ds(half, half)),
        }
        at, rows = where[kind]
        n = base + ("right", "left", "far_right", "far_left").index(kind)
        return pltpu.make_async_remote_copy(
            src_ref=buffer.at[at, rows],
            dst_ref=buffer.at[at, rows],
            send_sem=ad_send.at[n],
            recv_sem=ad_recv.at[n],
            device_id=at_x(1),
            device_id_type=MESH,
        )

    load_d.wait()
    d_all[x] = down_v[...].astype(BF16)
    share(d_all, 0, "right").start()
    share(d_all, 0, "left").start()

    half_rows = (pl.ds(0, ROWS // 2), pl.ds(ROWS // 2, ROWS // 2))

    def ring(direction, step, half):
        source, landing, way = ((sp, rp, 1), (sm, rm, -1))[direction]
        return pltpu.make_async_remote_copy(
            src_ref=source.at[step, half_rows[half]],
            dst_ref=landing.at[step, half_rows[half]],
            send_sem=rs_send.at[direction, step, half],
            recv_sem=rs_recv.at[direction, step, half],
            device_id=at_row(way),
            device_id_type=MESH,
        )

    load_s.wait()
    take_a.wait_recv()

    def base_block(i, carry):
        load_w(i).wait()
        columns = pl.ds(pl.multiple_of(block_of(i) * FEAT, FEAT), FEAT)
        scale = jnp.exp2(scl_v[:, columns].astype(F32)).astype(BF16)
        weight = (w_v[i].reshape(32, 32, FEAT) * scale[:, None, :]).reshape(2 * FEAT, FEAT)
        value = jnp.dot(a_all[0], weight[:FEAT], preferred_element_type=F32)
        value += jnp.dot(a_all[1], weight[FEAT:], preferred_element_type=F32)
        part[i] = value

        @pl.when(i == 0)
        def _():
            sp[0, half_rows[0]] = part[0, half_rows[0]].astype(BF16)
            ring(0, 0, 0).start()
            sm[0, half_rows[1]] = part[0, half_rows[1]].astype(BF16)
            ring(1, 0, 1).start()

        @pl.when(i == 1)
        def _():
            sp[1, half_rows[1]] = part[1, half_rows[1]].astype(BF16)
            ring(0, 1, 1).start()

        @pl.when(i == 2)
        def _():
            sm[1, half_rows[0]] = part[2, half_rows[0]].astype(BF16)
            ring(1, 1, 0).start()

        return carry

    lax.fori_loop(0, NROW, base_block, 0)

    load_u.wait()
    for q in range(FEAT // 128):
        u_all[x, :, q * 128 : (q + 1) * 128] = up_v[pl.ds(q, AD * RANK, stride=4), :].astype(BF16)
    arrived(d_all, 0, "right").wait_recv()
    share(d_all, 0, "far_right").start()
    arrived(d_all, 0, "left").wait_recv()
    share(d_all, 0, "far_left").start()
    share(u_all, 4, "right").start()
    share(u_all, 4, "left").start()

    def ring_step(direction, step, half):
        ring(direction, step - 1, half).wait_recv()
        source, landing, _ = ((sp, rp, 1), (sm, rm, -1))[direction]
        rows = half_rows[half]
        own = part[2 * step - 1 + direction, rows]
        source[step, rows] = (landing[step - 1, rows].astype(F32) + own).astype(BF16)
        ring(direction, step, half).start()

    ring_step(0, 1, 0)
    ring_step(1, 1, 1)
    for step in (2, 3):
        ring_step(0, step, 1)
        ring_step(1, step, 0)
        ring_step(0, step, 0)
        ring_step(1, step, 1)
        if step == 2:
            arrived(u_all, 4, "right").wait_recv()
            share(u_all, 4, "far_right").start()
            arrived(u_all, 4, "left").wait_recv()
            share(u_all, 4, "far_left").start()

    lane = lax.broadcasted_iota(I32, (BLK // 2, 128), 1)
    eye = lax.broadcasted_iota(I32, (BLK, 128), 0) == lax.broadcasted_iota(I32, (BLK, 128), 1)
    lane_adapter = (lax.broadcasted_iota(I32, (BLK, SLAB_W), 1) // RANK + 1).astype(F32)

    def adapter_mask(q):
        wanted = jnp.sum(jnp.where(eye, ids_r[q], 0.0), axis=1, keepdims=True)
        return lane_adapter == wanted

    def to_reducer(q):
        return pltpu.make_async_remote_copy(
            src_ref=low_s.at[q],
            dst_ref=red.at[flat],
            send_sem=low_send.at[q],
            recv_sem=red_recv.at[flat],
            device_id=(g, q // 2, q % 2),
            device_id_type=MESH,
        )

    def from_device(i):
        return pltpu.make_async_remote_copy(
            src_ref=red.at[i],
            dst_ref=red.at[i],
            send_sem=low_send.at[0],
            recv_sem=red_recv.at[i],
            device_id=(g, (r + 1) % NROW, c),
            device_id_type=MESH,
        )

    def to_all(q, i):
        return pltpu.make_async_remote_copy(
            src_ref=low_full.at[q],
            dst_ref=low_full.at[q],
            send_sem=full_send.at[i],
            recv_sem=full_recv.at[q],
            device_id=(g, (r + i // 2) % NROW, (c + i % 2) % 2),
            device_id_type=MESH,
        )

    for first, last in CHUNKS:
        rows = slice(first * BLK, last * BLK)
        for q in range(first, last):
            if q > 0:
                send_ids(q).wait_recv()
                send_rows(q).wait_recv()
        if first == 0:
            arrived(d_all, 0, "far_right").wait_recv()
            arrived(d_all, 0, "far_left").wait_recv()
        projected = lax.dot_general(
            xr[rows],
            d_all[...].reshape(SLAB_W, FEAT),
            (((1,), (1,)), ((), ())),
            preferred_element_type=F32,
        )
        for q in range(first, last):
            block = projected[(q - first) * BLK : (q - first + 1) * BLK]
            block = jnp.where(adapter_mask(q), block, 0.0)
            folded = block[:, 0:128]
            for k in range(1, SLAB_W // 128):
                folded += block[:, k * 128 : (k + 1) * 128]
            folded += pltpu.roll(folded, RANK, 1)
            low_s[q] = jnp.where(lane < RANK, folded[: BLK // 2], folded[BLK // 2 :])

            @pl.when(flat != q)
            def _():
                to_reducer(q).start()

            @pl.when(flat == q)
            def _():
                red[flat] = low_s[q]

        for q in range(first, last):

            @pl.when(flat == q)
            def _():
                for i in range(NFLAT):
                    if i != q:
                        from_device(i).wait_recv()
                total = red[0]
                for i in range(1, NFLAT):
                    total += red[i]
                low_full[q] = total

                def hand_out(i, carry):
                    to_all(q, i).start()
                    return carry

                lax.fori_loop(1, NFLAT, hand_out, 0)

        if first == 0:
            arrived(u_all, 4, "far_right").wait_recv()
            arrived(u_all, 4, "far_left").wait_recv()
        spread = []
        for q in range(first, last):

            @pl.when(flat != q)
            def _():
                to_all(q, 1).wait_recv()

            packed = low_full[q]
            turned = pltpu.roll(packed, RANK, 1)
            both = jnp.concatenate(
                [jnp.where(lane < RANK, packed, turned), jnp.where(lane < RANK, turned, packed)],
                axis=0,
            )
            wide = jnp.concatenate([both] * (SLAB_W // 128), axis=1)
            spread.append(jnp.where(adapter_mask(q), wide, 0.0).astype(BF16))
        delta = jnp.dot(
            jnp.concatenate(spread, axis=0),
            u_all[...].reshape(SLAB_W, FEAT),
            preferred_element_type=F32,
        ).astype(BF16)
        back_s[rows] = delta
        for q in range(first, last):
            if q > 0:
                send_back(q).start()
            else:
                back_r[0:BLK] = delta[0:BLK]

    for half in (1, 0):
        ring(0, 3, half).wait_recv()
        ring(1, 3, 1 - half).wait_recv()
    acc[...] = part[7] + (rp[3].astype(F32) + rm[3].astype(F32))

    for q in range(1, NZ):
        send_back(q).wait_recv()
    added = lax.dot_general(
        choose[...], back_r[...], (((0,), (0,)), ((), ())), preferred_element_type=F32
    )
    out_ref[...] = (acc[...] + added).astype(BF16)

    swap_a.wait_send()
    for q in range(1, NZ):
        send_ids(q).wait_send()
        send_rows(q).wait_send()
        send_back(q).wait_send()
    for buffer, base in ((d_all, 0), (u_all, 4)):
        for kind in ("right", "left", "far_right", "far_left"):
            share(buffer, base, kind).wait_send()
    for direction in (0, 1):
        ring(direction, 0, direction).wait_send()
        for step in (1, 2, 3):
            for half in (0, 1):
                ring(direction, step, half).wait_send()
    for q in range(NZ):

        @pl.when(flat != q)
        def _():
            to_reducer(q).wait_send()

        @pl.when(flat == q)
        def _():
            def left(i, carry):
                to_all(q, i).wait_send()
                return carry

            lax.fori_loop(1, NFLAT, left, 0)


def per_device(
    activations,
    base_weight_codes,
    block_scale_exponents,
    adapter_down_weight,
    adapter_up_weight,
    row_adapter_index,
    adapter_storage_slot,
):
    down = jnp.transpose(adapter_down_weight, (0, 2, 1)).reshape(AD * RANK, FEAT)
    up = adapter_up_weight.reshape(AD * RANK * FEAT // 128, 128)
    hbm = pl.BlockSpec(memory_space=pl.ANY)
    vmem = pl.BlockSpec(memory_space=pltpu.VMEM)
    dma = pltpu.SemaphoreType.DMA
    padded = NZ * BLK
    out = pl.pallas_call(
        kernel,
        out_shape=jax.ShapeDtypeStruct((ROWS, FEAT), BF16),
        in_specs=[hbm] * 5 + [vmem] * 2,
        out_specs=vmem,
        scratch_shapes=[
            pltpu.VMEM((2, ROWS, FEAT), BF16),
            pltpu.VMEM((NROW, 2 * FEAT, FEAT), BF16),
            pltpu.VMEM((32, NROW * FEAT), I32),
            pltpu.VMEM((AD * RANK, FEAT), F32),
            pltpu.VMEM((AD * RANK * FEAT // 128, 128), F32),
            pltpu.VMEM((1, 256), F32),
            pltpu.VMEM((padded, ROWS), BF16),
            pltpu.VMEM((padded, FEAT), BF16),
            pltpu.VMEM((padded, FEAT), BF16),
            pltpu.VMEM((NZ, 1, 128), F32),
            pltpu.VMEM((NZ, 1, 128), F32),
            pltpu.VMEM((NX, AD * RANK, FEAT), BF16),
            pltpu.VMEM((NX, AD * RANK, FEAT), BF16),
            pltpu.VMEM((NROW, ROWS, FEAT), F32),
            pltpu.VMEM((4, ROWS, FEAT), BF16),
            pltpu.VMEM((4, ROWS, FEAT), BF16),
            pltpu.VMEM((4, ROWS, FEAT), BF16),
            pltpu.VMEM((4, ROWS, FEAT), BF16),
            pltpu.VMEM((NZ, BLK // 2, 128), F32),
            pltpu.VMEM((NFLAT, BLK // 2, 128), F32),
            pltpu.VMEM((NZ, BLK // 2, 128), F32),
            pltpu.VMEM((padded, FEAT), BF16),
            pltpu.VMEM((padded, FEAT), BF16),
            pltpu.VMEM((ROWS, FEAT), F32),
            dma((4,)),
            dma((NROW,)),
            dma((2,)),
            dma((NZ,)),
            dma((NZ,)),
            dma((NZ,)),
            dma((NZ,)),
            dma((8,)),
            dma((8,)),
            dma((2, 4, 2)),
            dma((2, 4, 2)),
            dma((NZ,)),
            dma((NFLAT,)),
            dma((NFLAT,)),
            dma((NZ,)),
            dma((NZ,)),
            dma((NZ,)),
        ],
        compiler_params=pltpu.CompilerParams(
            collective_id=0, has_side_effects=True, vmem_limit_bytes=56 * 1024 * 1024
        ),
        cost_estimate=pl.CostEstimate(
            flops=2 * ROWS * 2 * FEAT * NROW * FEAT, bytes_accessed=11 << 20, transcendentals=0
        ),
        name="projection",
    )(
        activations,
        base_weight_codes,
        block_scale_exponents,
        down,
        up,
        row_adapter_index.reshape(1, ROWS),
        adapter_storage_slot.reshape(1, -1),
    )
    return out.reshape(ROWS, 1, 1, FEAT)


def solution(mesh):
    return jax.shard_map(
        per_device,
        mesh=mesh,
        in_specs=(
            P("group", ("row", "col")),
            P("row", "col"),
            P("row", "col"),
            P("group", ("row", "col"), None),
            P("group", None, "col", "row", None),
            P("group"),
            P(),
        ),
        out_specs=P("group", "col", "row", None),
        check_vma=False,
    )
```

time: 261 us -> 87 us (0.33); the launches traced: 256 us -> 85.9 us
  waiting for transfers between devices: 140 us -> 0 us
  Pallas kernels: 0 us -> 84.2 us
  blocking collectives: 46 us -> 0 us
  starting transfers between devices: 23.5 us -> 0 us
  between operations: 15 us -> 0.01 us
  matrix products: 13.4 us -> 0 us
  other arithmetic: 11 us -> 0 us
  local copies, waits for them, and re-layouts: 6.46 us -> 1.67 us
    psum x1 -> x0, waiting for transfers between devices: 117 us -> none  [per_device(): spread_rows = lax.psum(spread_part, ('row', 'col'))]
    pallas_call x0 -> x1, Pallas kernels: none -> 84.2 us  [per_device(): pl.pallas_call(kernel, out_shape=jax.ShapeDtypeStruct((ROWS, FEAT), BF16)...]
    all_to_all x1 -> x0, blocking collectives: 42.1 us -> none  [per_device(): lax.all_to_all(adapter_delta, 'group', split_axis=0, concat_axis=0, tiled...]
    all_to_all x2 -> x0, starting transfers between devices: 23.4 us -> none  [the longest x1 18.8 us: per_device(): lax.all_to_all(send_ids, 'group', split_axis=0, concat_axis=0, tiled=True)]
    all_to_all x2 -> x0, waiting for transfers between devices: 23.4 us -> none  [the longest x1 14.7 us: per_device(): lax.all_to_all(send_rows, 'group', split_axis=0, concat_axis=0, tiled=True)]
    dot_general x5 -> x0, matrix products: 13.4 us -> none  [the longest x1 5.89 us: per_device(): jnp.dot(lax.all_gather(activations, 'col', axis=1, tiled=True), weight, p...]
    mul x1 -> x0, other arithmetic: 7.34 us -> none  [per_device(): base_weight_codes.reshape(inputs_here // 32, 32, outputs_here)]
    all_gather x1 -> x0, blocking collectives: 3.9 us -> none  [per_device(): lax.all_gather(activations, 'col', axis=1, tiled=True)]
  transfers between devices with their start and end apart: 4 -> 0, of which waited for: 3 -> 0; matrix products, arithmetic and copies ran while one was open for 9% -> 0% of each run, Pallas kernels for 0% -> 0%
where the time goes in v1:
time: 87 us; the launch traced here: 85.9 us
  Pallas kernels  84.2 us (97%)
  local copies, waits for them, and re-layouts  1.67 us (2%)
    pallas_call x1, Pallas kernels, per_device(): pl.pallas_call(kernel, out_shape=jax.ShapeDtypeStruct((ROWS, FEAT), BF16)...  84.2 us

profile of v1, /device:TPU:1, one launch (start us, length us, event | category | flops | bytes accessed | tf_op | source)
XLA Modules:
  0.0 85.9 jit_solution(9501268328086006125)
XLA Ops:
  0.0 84.2 %projection.1 = bf16[256,512]{1,0:T(8,128)(2,1)} custom-call(bf16[256,512]{1,0:T(8,128)(2,1)} %act_h.1, bf16[1024,4096]{1,0:T(8,128)(2,1)} %codes_h.1, s32[32,4096]{1,0:T(8,128)} %scl_h.1, f32[256,512]{1,0:T(8,128)} %bitcast.8, f32[1024,128]{1,0:T(8,128)} %bitcast.9, s32[1,256]{1,0:T(1,128)} %bitcast.10, s32[1,192]{1,0:T(1,128)} %bitcast.11), custom_call_target="tpu_custom_call" | custom-call | flops 2147483648 | bytes 11534336 | tf_op jit(solution)/shard_map/projection/pallas_call | solution.py:527
  84.2 1.7 %copy.9 = bf16[256,1,1,512]{3,0,2,1:T(8,128)(2,1)} copy(bf16[256,1,1,512]{3,0,2,1:T(8,128)(2,1)} %bitcast.7) | data formatting | bytes 524288

commit v2 on v1

--- a/solution.py
+++ b/solution.py
@@ -23,8 +23,7 @@
 AD = 4
 SLAB_W = NX * AD * RANK
 
-ORDER = (0, 1, 11, 2, 10, 3, 9, 4, 8, 5, 7, 6)
-CHUNKS = ((0, 12),)
+CHUNKS = ((0, 4), (4, 8), (8, 12))
 
 
 def kernel(
@@ -77,6 +76,7 @@
     full_recv,
     b_send,
     b_recv,
+    hello,
 ):
     g = lax.axis_index("group")
     r = lax.axis_index("row")
@@ -85,8 +85,8 @@
     z = g % NZ
     flat = 2 * r + c
 
-    def at_z(offset):
-        return (x * NZ + (z + offset + NZ) % NZ, r, c)
+    def at_z(there):
+        return (x * NZ + there, r, c)
 
     def at_x(offset):
         return (((x + offset + NX) % NX) * NZ + z, r, c)
@@ -115,10 +115,12 @@
     load_u.start()
 
     barrier = pltpu.get_barrier_semaphore()
-    peers = [at_z(o) for o in range(1, NZ)]
-    peers += [at_x(o) for o in range(1, NX)]
-    for device in peers:
-        pl.semaphore_signal(barrier, inc=1, device_id=device, device_id_type=MESH)
+    for o in range(1, NX):
+        pl.semaphore_signal(barrier, inc=1, device_id=at_x(o), device_id_type=MESH)
+
+    def greet_later(there, carry):
+        pl.semaphore_signal(barrier, inc=1, device_id=at_z(there), device_id_type=MESH)
+        return carry
 
     def greet(i, carry):
         pl.semaphore_signal(
@@ -130,6 +132,7 @@
         return carry
 
     lax.fori_loop(1, NFLAT, greet, 0)
+    lax.fori_loop(z + 1, NZ, greet_later, 0)
 
     tab_v[...] = jnp.zeros(tab_v.shape, F32)
     tab_v[:, : tab_ref.shape[1]] = tab_ref[...].astype(F32)
@@ -142,11 +145,7 @@
     owner_x = (
         (owner >= NZ).astype(I32) + (owner >= 2 * NZ).astype(I32) + (owner >= 3 * NZ).astype(I32)
     )
-    away = z - (owner - NZ * owner_x)
-    away = jnp.where(away < 0, away + NZ, away)
-    place = jnp.zeros_like(away)
-    for q, o in enumerate(ORDER):
-        place = jnp.where(away == o, q, place)
+    place = owner - NZ * owner_x
     adapter = (owner_x * AD + (slots & 3) + 1).astype(F32).astype(BF16)
     sent_to = lax.broadcasted_iota(I32, (16, ROWS), 0) == place[0:1]
     before = (
@@ -159,56 +158,14 @@
     )
     position = jnp.sum(jnp.where(sent_to, prefix, 0.0), axis=0, keepdims=True).astype(I32)
     target = place[0:1] * BLK + position
-    choose[...] = (
-        (lax.broadcasted_iota(I32, (NZ * BLK, ROWS), 0) == target).astype(F32).astype(BF16)
-    )
-    ids_s[...] = jnp.zeros(ids_s.shape, F32)
-    for q in range(NZ):
-        row = lax.dot_general(
-            adapter,
-            choose[q * BLK : (q + 1) * BLK, :],
-            (((1,), (1,)), ((), ())),
-            preferred_element_type=F32,
-        )
-        ids_s[q, :, 0:BLK] = row[0:1]
-    ids_r[0] = ids_s[0]
-    load_a.wait()
-    xs[...] = jnp.dot(choose[...], a_all[c], preferred_element_type=F32).astype(BF16)
-    xr[0:BLK] = xs[0:BLK]
-
-    pl.semaphore_wait(barrier, len(peers) + NFLAT - 1)
-
-    def send_rows(q):
-        rows = pl.ds(q * BLK, BLK)
-        return pltpu.make_async_remote_copy(
-            src_ref=xs.at[rows],
-            dst_ref=xr.at[rows],
-            send_sem=x_send.at[q],
-            recv_sem=x_recv.at[q],
-            device_id=at_z(-ORDER[q]),
-            device_id_type=MESH,
-        )
-
-    def send_ids(q):
-        return pltpu.make_async_remote_copy(
-            src_ref=ids_s.at[q],
-            dst_ref=ids_r.at[q],
-            send_sem=i_send.at[q],
-            recv_sem=i_recv.at[q],
-            device_id=at_z(-ORDER[q]),
-            device_id_type=MESH,
-        )
-
-    def send_back(q):
-        rows = pl.ds(q * BLK, BLK)
-        return pltpu.make_async_remote_copy(
-            src_ref=back_s.at[rows],
-            dst_ref=back_r.at[rows],
-            send_sem=b_send.at[q],
-            recv_sem=b_recv.at[q],
-            device_id=at_z(ORDER[q]),
-            device_id_type=MESH,
-        )
+
+    pl.semaphore_wait(barrier, NX - 1 + NFLAT - 1 + z)
+
+    def greet_earlier(there, carry):
+        pl.semaphore_signal(hello.at[z], inc=1, device_id=at_z(there), device_id_type=MESH)
+        return carry
+
+    lax.fori_loop(0, z, greet_earlier, 0)
 
     swap_a = pltpu.make_async_remote_copy(
         src_ref=a_all.at[c],
@@ -226,10 +183,6 @@
         device_id=(g, r, 1 - c),
         device_id_type=MESH,
     )
-    swap_a.start()
-    for q in range(1, NZ):
-        send_ids(q).start()
-        send_rows(q).start()
 
     def share(buffer, base, kind):
         half = AD * RANK // 2
@@ -268,11 +221,107 @@
             device_id=at_x(1),
             device_id_type=MESH,
         )
-
     load_d.wait()
     d_all[x] = down_v[...].astype(BF16)
     share(d_all, 0, "right").start()
     share(d_all, 0, "left").start()
+    load_a.wait()
+    swap_a.start()
+
+    choose[...] = (
+        (lax.broadcasted_iota(I32, (NZ * BLK, ROWS), 0) == target).astype(F32).astype(BF16)
+    )
+    ids_s[...] = jnp.zeros(ids_s.shape, F32)
+    for q in range(NZ):
+        row = lax.dot_general(
+            adapter,
+            choose[q * BLK : (q + 1) * BLK, :],
+            (((1,), (1,)), ((), ())),
+            preferred_element_type=F32,
+        )
+        ids_s[q, :, 0:BLK] = row[0:1]
+    ids_r[z] = ids_s[z]
+    xs[...] = (
+        jnp.dot(choose[...], a_all[c], preferred_element_type=F32)
+        .astype(BF16)
+        .reshape(NZ, BLK, FEAT)
+    )
+    xr[z] = xs[z]
+
+    def send_rows(there):
+        return pltpu.make_async_remote_copy(
+            src_ref=xs.at[there],
+            dst_ref=xr.at[z],
+            send_sem=x_send.at[there],
+            recv_sem=x_recv.at[z],
+            device_id=at_z(there),
+            device_id_type=MESH,
+        )
+
+    def take_rows(there):
+        return pltpu.make_async_remote_copy(
+            src_ref=xr.at[there],
+            dst_ref=xr.at[there],
+            send_sem=x_send.at[there],
+            recv_sem=x_recv.at[there],
+            device_id=at_z(there),
+            device_id_type=MESH,
+        )
+
+    def send_ids(there):
+        return pltpu.make_async_remote_copy(
+            src_ref=ids_s.at[there],
+            dst_ref=ids_r.at[z],
+            send_sem=i_send.at[there],
+            recv_sem=i_recv.at[z],
+            device_id=at_z(there),
+            device_id_type=MESH,
+        )
+
+    def take_ids(there):
+        return pltpu.make_async_remote_copy(
+            src_ref=ids_r.at[there],
+            dst_ref=ids_r.at[there],
+            send_sem=i_send.at[there],
+            recv_sem=i_recv.at[there],
+            device_id=at_z(there),
+            device_id_type=MESH,
+        )
+
+    def send_back(there):
+        return pltpu.make_async_remote_copy(
+            src_ref=back_s.at[there],
+            dst_ref=back_r.at[z],
+            send_sem=b_send.at[there],
+            recv_sem=b_recv.at[z],
+            device_id=at_z(there),
+            device_id_type=MESH,
+        )
+
+    def take_back(there):
+        return pltpu.make_async_remote_copy(
+            src_ref=back_r.at[there],
+            dst_ref=back_r.at[there],
+            send_sem=b_send.at[there],
+            recv_sem=b_recv.at[there],
+            device_id=at_z(there),
+            device_id_type=MESH,
+        )
+
+    def post_earlier(k, carry):
+        there = jnp.where(k % 2 == 0, k // 2, z - 1 - k // 2)
+        send_ids(there).start()
+        send_rows(there).start()
+        return carry
+
+    lax.fori_loop(0, z, post_earlier, 0)
+
+    def post_later(there):
+        @pl.when(there < NZ)
+        def _():
+            pl.semaphore_wait(hello.at[there], 1)
+            send_ids(there).start()
+            send_rows(there).start()
 
     half_rows = (pl.ds(0, ROWS // 2), pl.ds(ROWS // 2, ROWS // 2))
 
@@ -316,9 +365,12 @@
             sm[1, half_rows[0]] = part[2, half_rows[0]].astype(BF16)
             ring(1, 1, 0).start()
 
+        post_later(z + 1 + i)
         return carry
 
     lax.fori_loop(0, NROW, base_block, 0)
+    for later in range(NROW + 1, NZ):
+        post_later(z + later)
 
     load_u.wait()
     for q in range(FEAT // 128):
@@ -338,19 +390,6 @@
         source[step, rows] = (landing[step - 1, rows].astype(F32) + own).astype(BF16)
         ring(direction, step, half).start()
 
-    ring_step(0, 1, 0)
-    ring_step(1, 1, 1)
-    for step in (2, 3):
-        ring_step(0, step, 1)
-        ring_step(1, step, 0)
-        ring_step(0, step, 0)
-        ring_step(1, step, 1)
-        if step == 2:
-            arrived(u_all, 4, "right").wait_recv()
-            share(u_all, 4, "far_right").start()
-            arrived(u_all, 4, "left").wait_recv()
-            share(u_all, 4, "far_left").start()
-
     lane = lax.broadcasted_iota(I32, (BLK // 2, 128), 1)
     eye = lax.broadcasted_iota(I32, (BLK, 128), 0) == lax.broadcasted_iota(I32, (BLK, 128), 1)
     lane_adapter = (lax.broadcasted_iota(I32, (BLK, SLAB_W), 1) // RANK + 1).astype(F32)
@@ -389,17 +428,17 @@
             device_id_type=MESH,
         )
 
-    for first, last in CHUNKS:
-        rows = slice(first * BLK, last * BLK)
+    def project(chunk):
+        first, last = chunk
         for q in range(first, last):
-            if q > 0:
-                send_ids(q).wait_recv()
-                send_rows(q).wait_recv()
-        if first == 0:
-            arrived(d_all, 0, "far_right").wait_recv()
-            arrived(d_all, 0, "far_left").wait_recv()
+
+            @pl.when(z != q)
+            def _():
+                take_ids(q).wait_recv()
+                take_rows(q).wait_recv()
+
         projected = lax.dot_general(
-            xr[rows],
+            xr[first:last].reshape((last - first) * BLK, FEAT),
             d_all[...].reshape(SLAB_W, FEAT),
             (((1,), (1,)), ((), ())),
             preferred_element_type=F32,
@@ -421,7 +460,8 @@
             def _():
                 red[flat] = low_s[q]
 
-        for q in range(first, last):
+    def reduce_low(chunk):
+        for q in range(*chunk):
 
             @pl.when(flat == q)
             def _():
@@ -439,9 +479,8 @@
 
                 lax.fori_loop(1, NFLAT, hand_out, 0)
 
-        if first == 0:
-            arrived(u_all, 4, "far_right").wait_recv()
-            arrived(u_all, 4, "far_left").wait_recv()
+    def expand(chunk):
+        first, last = chunk
         spread = []
         for q in range(first, last):
 
@@ -462,30 +501,73 @@
             u_all[...].reshape(SLAB_W, FEAT),
             preferred_element_type=F32,
         ).astype(BF16)
-        back_s[rows] = delta
+        back_s[first:last] = delta.reshape(last - first, BLK, FEAT)
         for q in range(first, last):
-            if q > 0:
+
+            @pl.when(z != q)
+            def _():
                 send_back(q).start()
-            else:
-                back_r[0:BLK] = delta[0:BLK]
+
+            @pl.when(z == q)
+            def _():
+                back_r[q] = back_s[q]
+
+    ring_step(0, 1, 0)
+    ring_step(1, 1, 1)
+    arrived(d_all, 0, "far_right").wait_recv()
+    arrived(d_all, 0, "far_left").wait_recv()
+    project(CHUNKS[0])
+    ring_step(0, 2, 1)
+    ring_step(1, 2, 0)
+    ring_step(0, 2, 0)
+    ring_step(1, 2, 1)
+    reduce_low(CHUNKS[0])
+    arrived(u_all, 4, "right").wait_recv()
+    share(u_all, 4, "far_right").start()
+    arrived(u_all, 4, "left").wait_recv()
+    share(u_all, 4, "far_left").start()
+    project(CHUNKS[1])
+    arrived(u_all, 4, "far_right").wait_recv()
+    arrived(u_all, 4, "far_left").wait_recv()
+    expand(CHUNKS[0])
+    ring_step(0, 3, 1)
+    ring_step(1, 3, 0)
+    ring_step(0, 3, 0)
+    ring_step(1, 3, 1)
+    reduce_low(CHUNKS[1])
+    expand(CHUNKS[1])
+    project(CHUNKS[2])
+    reduce_low(CHUNKS[2])
+    expand(CHUNKS[2])
 
     for half in (1, 0):
         ring(0, 3, half).wait_recv()
         ring(1, 3, 1 - half).wait_recv()
     acc[...] = part[7] + (rp[3].astype(F32) + rm[3].astype(F32))
 
-    for q in range(1, NZ):
-        send_back(q).wait_recv()
+    for q in range(NZ):
+
+        @pl.when(z != q)
+        def _():
+            take_back(q).wait_recv()
+
     added = lax.dot_general(
-        choose[...], back_r[...], (((0,), (0,)), ((), ())), preferred_element_type=F32
+        choose[...],
+        back_r[...].reshape(NZ * BLK, FEAT),
+        (((0,), (0,)), ((), ())),
+        preferred_element_type=F32,
     )
     out_ref[...] = (acc[...] + added).astype(BF16)
 
     swap_a.wait_send()
-    for q in range(1, NZ):
-        send_ids(q).wait_send()
-        send_rows(q).wait_send()
-        send_back(q).wait_send()
+    for q in range(NZ):
+
+        @pl.when(z != q)
+        def _():
+            send_ids(q).wait_send()
+            send_rows(q).wait_send()
+            send_back(q).wait_send()
+
     for buffer, base in ((d_all, 0), (u_all, 4)):
         for kind in ("right", "left", "far_right", "far_left"):
             share(buffer, base, kind).wait_send()
@@ -537,8 +619,8 @@
             pltpu.VMEM((AD * RANK * FEAT // 128, 128), F32),
             pltpu.VMEM((1, 256), F32),
             pltpu.VMEM((padded, ROWS), BF16),
-            pltpu.VMEM((padded, FEAT), BF16),
-            pltpu.VMEM((padded, FEAT), BF16),
+            pltpu.VMEM((NZ, BLK, FEAT), BF16),
+            pltpu.VMEM((NZ, BLK, FEAT), BF16),
             pltpu.VMEM((NZ, 1, 128), F32),
             pltpu.VMEM((NZ, 1, 128), F32),
             pltpu.VMEM((NX, AD * RANK, FEAT), BF16),
@@ -551,8 +633,8 @@
             pltpu.VMEM((NZ, BLK // 2, 128), F32),
             pltpu.VMEM((NFLAT, BLK // 2, 128), F32),
             pltpu.VMEM((NZ, BLK // 2, 128), F32),
-            pltpu.VMEM((padded, FEAT), BF16),
-            pltpu.VMEM((padded, FEAT), BF16),
+            pltpu.VMEM((NZ, BLK, FEAT), BF16),
+            pltpu.VMEM((NZ, BLK, FEAT), BF16),
             pltpu.VMEM((ROWS, FEAT), F32),
             dma((4,)),
             dma((NROW,)),
@@ -571,6 +653,7 @@
             dma((NZ,)),
             dma((NZ,)),
             dma((NZ,)),
+            pltpu.SemaphoreType.REGULAR((NZ,)),
         ],
         compiler_params=pltpu.CompilerParams(
             collective_id=0, has_side_effects=True, vmem_limit_bytes=56 * 1024 * 1024

time: 87 us -> 89.4 us (1.028); the launches traced: 85.9 us -> 89.2 us
  Pallas kernels: 84.2 us -> 87.5 us
    pallas_call x1, Pallas kernels: 84.2 us -> 87.5 us  [per_device(): pl.pallas_call(kernel, out_shape=jax.ShapeDtypeStruct((ROWS, FEAT), BF16)...]
where the time goes in v2:
time: 89.4 us; the launch traced here: 89.2 us
  Pallas kernels  87.5 us (98%)
  local copies, waits for them, and re-layouts  1.67 us (2%)
    pallas_call x1, Pallas kernels, per_device(): pl.pallas_call(kernel, out_shape=jax.ShapeDtypeStruct((ROWS, FEAT), BF16)...  87.5 us

profile of v2, /device:TPU:1, one launch (start us, length us, event | category | flops | bytes accessed | tf_op | source)
XLA Modules:
  0.0 89.2 jit_solution(9233890988418195364)
XLA Ops:
  0.0 87.5 %projection.1 = bf16[256,512]{1,0:T(8,128)(2,1)} custom-call(bf16[256,512]{1,0:T(8,128)(2,1)} %act_h.1, bf16[1024,4096]{1,0:T(8,128)(2,1)} %codes_h.1, s32[32,4096]{1,0:T(8,128)} %scl_h.1, f32[256,512]{1,0:T(8,128)} %bitcast.8, f32[1024,128]{1,0:T(8,128)} %bitcast.9, s32[1,256]{1,0:T(1,128)} %bitcast.10, s32[1,192]{1,0:T(1,128)} %bitcast.11), custom_call_target="tpu_custom_call" | custom-call | flops 2147483648 | bytes 11534336 | tf_op jit(solution)/shard_map/projection/pallas_call | solution.py:609
  87.5 1.7 %copy.9 = bf16[256,1,1,512]{3,0,2,1:T(8,128)(2,1)} copy(bf16[256,1,1,512]{3,0,2,1:T(8,128)(2,1)} %bitcast.7) | data formatting | bytes 524288

commit v3 on v2

--- a/solution.py
+++ b/solution.py
@@ -23,7 +23,7 @@
 AD = 4
 SLAB_W = NX * AD * RANK
 
-CHUNKS = ((0, 4), (4, 8), (8, 12))
+CHUNKS = ((0, 6), (6, 12))
 
 
 def kernel(
@@ -134,6 +134,14 @@
     lax.fori_loop(1, NFLAT, greet, 0)
     lax.fori_loop(z + 1, NZ, greet_later, 0)
 
+    pl.semaphore_wait(barrier, NX - 1 + NFLAT - 1 + z)
+
+    def greet_earlier(there, carry):
+        pl.semaphore_signal(hello.at[z], inc=1, device_id=at_z(there), device_id_type=MESH)
+        return carry
+
+    lax.fori_loop(0, z, greet_earlier, 0)
+
     tab_v[...] = jnp.zeros(tab_v.shape, F32)
     tab_v[:, : tab_ref.shape[1]] = tab_ref[...].astype(F32)
     ids = ids_ref[...]
@@ -159,14 +167,6 @@
     position = jnp.sum(jnp.where(sent_to, prefix, 0.0), axis=0, keepdims=True).astype(I32)
     target = place[0:1] * BLK + position
 
-    pl.semaphore_wait(barrier, NX - 1 + NFLAT - 1 + z)
-
-    def greet_earlier(there, carry):
-        pl.semaphore_signal(hello.at[z], inc=1, device_id=at_z(there), device_id_type=MESH)
-        return carry
-
-    lax.fori_loop(0, z, greet_earlier, 0)
-
     swap_a = pltpu.make_async_remote_copy(
         src_ref=a_all.at[c],
         dst_ref=a_all.at[c],
@@ -398,13 +398,21 @@
         wanted = jnp.sum(jnp.where(eye, ids_r[q], 0.0), axis=1, keepdims=True)
         return lane_adapter == wanted
 
-    def to_reducer(q):
-        return pltpu.make_async_remote_copy(
-            src_ref=low_s.at[q],
+    def reducer(p):
+        return (3 * p) % NROW, p % 2
+
+    def adds_up(p):
+        row, col = reducer(p)
+        return flat == 2 * row + col
+
+    def to_reducer(p):
+        row, col = reducer(p)
+        return pltpu.make_async_remote_copy(
+            src_ref=low_s.at[p],
             dst_ref=red.at[flat],
-            send_sem=low_send.at[q],
+            send_sem=low_send.at[p],
             recv_sem=red_recv.at[flat],
-            device_id=(g, q // 2, q % 2),
+            device_id=(g, row, col),
             device_id_type=MESH,
         )
 
@@ -418,12 +426,12 @@
             device_id_type=MESH,
         )
 
-    def to_all(q, i):
-        return pltpu.make_async_remote_copy(
-            src_ref=low_full.at[q],
-            dst_ref=low_full.at[q],
+    def to_all(p, i):
+        return pltpu.make_async_remote_copy(
+            src_ref=low_full.at[p],
+            dst_ref=low_full.at[p],
             send_sem=full_send.at[i],
-            recv_sem=full_recv.at[q],
+            recv_sem=full_recv.at[p],
             device_id=(g, (r + i // 2) % NROW, (c + i % 2) % 2),
             device_id_type=MESH,
         )
@@ -443,38 +451,42 @@
             (((1,), (1,)), ((), ())),
             preferred_element_type=F32,
         )
-        for q in range(first, last):
-            block = projected[(q - first) * BLK : (q - first + 1) * BLK]
-            block = jnp.where(adapter_mask(q), block, 0.0)
-            folded = block[:, 0:128]
-            for k in range(1, SLAB_W // 128):
-                folded += block[:, k * 128 : (k + 1) * 128]
-            folded += pltpu.roll(folded, RANK, 1)
-            low_s[q] = jnp.where(lane < RANK, folded[: BLK // 2], folded[BLK // 2 :])
-
-            @pl.when(flat != q)
+        for p in range(first // 2, last // 2):
+            halves = []
+            for q in (2 * p, 2 * p + 1):
+                block = projected[(q - first) * BLK : (q - first + 1) * BLK]
+                block = jnp.where(adapter_mask(q), block, 0.0)
+                folded = block[:, 0:128]
+                for k in range(1, SLAB_W // 128):
+                    folded += block[:, k * 128 : (k + 1) * 128]
+                folded += pltpu.roll(folded, RANK, 1)
+                halves.append(jnp.where(lane < RANK, folded[: BLK // 2], folded[BLK // 2 :]))
+            low_s[p] = jnp.concatenate(halves, axis=0).astype(BF16)
+
+            @pl.when(jnp.logical_not(adds_up(p)))
             def _():
-                to_reducer(q).start()
-
-            @pl.when(flat == q)
+                to_reducer(p).start()
+
+            @pl.when(adds_up(p))
             def _():
-                red[flat] = low_s[q]
+                red[flat] = low_s[p]
 
     def reduce_low(chunk):
-        for q in range(*chunk):
-
-            @pl.when(flat == q)
+        for p in range(chunk[0] // 2, chunk[1] // 2):
+
+            @pl.when(adds_up(p))
             def _():
+                row, col = reducer(p)
                 for i in range(NFLAT):
-                    if i != q:
+                    if i != 2 * row + col:
                         from_device(i).wait_recv()
-                total = red[0]
+                total = red[0].astype(F32)
                 for i in range(1, NFLAT):
-                    total += red[i]
-                low_full[q] = total
+                    total += red[i].astype(F32)
+                low_full[p] = total.astype(BF16)
 
                 def hand_out(i, carry):
-                    to_all(q, i).start()
+                    to_all(p, i).start()
                     return carry
 
                 lax.fori_loop(1, NFLAT, hand_out, 0)
@@ -482,20 +494,25 @@
     def expand(chunk):
         first, last = chunk
         spread = []
-        for q in range(first, last):
-
-            @pl.when(flat != q)
+        for p in range(first // 2, last // 2):
+
+            @pl.when(jnp.logical_not(adds_up(p)))
             def _():
-                to_all(q, 1).wait_recv()
-
-            packed = low_full[q]
-            turned = pltpu.roll(packed, RANK, 1)
-            both = jnp.concatenate(
-                [jnp.where(lane < RANK, packed, turned), jnp.where(lane < RANK, turned, packed)],
-                axis=0,
-            )
-            wide = jnp.concatenate([both] * (SLAB_W // 128), axis=1)
-            spread.append(jnp.where(adapter_mask(q), wide, 0.0).astype(BF16))
+                to_all(p, 1).wait_recv()
+
+            summed = low_full[p].astype(F32)
+            for q in (2 * p, 2 * p + 1):
+                packed = summed[(q % 2) * (BLK // 2) : (q % 2 + 1) * (BLK // 2)]
+                turned = pltpu.roll(packed, RANK, 1)
+                both = jnp.concatenate(
+                    [
+                        jnp.where(lane < RANK, packed, turned),
+                        jnp.where(lane < RANK, turned, packed),
+                    ],
+                    axis=0,
+                )
+                wide = jnp.concatenate([both] * (SLAB_W // 128), axis=1)
+                spread.append(jnp.where(adapter_mask(q), wide, 0.0).astype(BF16))
         delta = jnp.dot(
             jnp.concatenate(spread, axis=0),
             u_all[...].reshape(SLAB_W, FEAT),
@@ -530,15 +547,12 @@
     arrived(u_all, 4, "far_right").wait_recv()
     arrived(u_all, 4, "far_left").wait_recv()
     expand(CHUNKS[0])
+    reduce_low(CHUNKS[1])
     ring_step(0, 3, 1)
     ring_step(1, 3, 0)
     ring_step(0, 3, 0)
     ring_step(1, 3, 1)
-    reduce_low(CHUNKS[1])
     expand(CHUNKS[1])
-    project(CHUNKS[2])
-    reduce_low(CHUNKS[2])
-    expand(CHUNKS[2])
 
     for half in (1, 0):
         ring(0, 3, half).wait_recv()
@@ -576,16 +590,16 @@
         for step in (1, 2, 3):
             for half in (0, 1):
                 ring(direction, step, half).wait_send()
-    for q in range(NZ):
-
-        @pl.when(flat != q)
+    for p in range(NZ // 2):
+
+        @pl.when(jnp.logical_not(adds_up(p)))
         def _():
-            to_reducer(q).wait_send()
-
-        @pl.when(flat == q)
+            to_reducer(p).wait_send()
+
+        @pl.when(adds_up(p))
         def _():
             def left(i, carry):
-                to_all(q, i).wait_send()
+                to_all(p, i).wait_send()
                 return carry
 
             lax.fori_loop(1, NFLAT, left, 0)
@@ -630,9 +644,9 @@
             pltpu.VMEM((4, ROWS, FEAT), BF16),
             pltpu.VMEM((4, ROWS, FEAT), BF16),
             pltpu.VMEM((4, ROWS, FEAT), BF16),
-            pltpu.VMEM((NZ, BLK // 2, 128), F32),
-            pltpu.VMEM((NFLAT, BLK // 2, 128), F32),
-            pltpu.VMEM((NZ, BLK // 2, 128), F32),
+            pltpu.VMEM((NZ // 2, BLK, 128), BF16),
+            pltpu.VMEM((NFLAT, BLK, 128), BF16),
+            pltpu.VMEM((NZ // 2, BLK, 128), BF16),
             pltpu.VMEM((NZ, BLK, FEAT), BF16),
             pltpu.VMEM((NZ, BLK, FEAT), BF16),
             pltpu.VMEM((ROWS, FEAT), F32),
@@ -647,10 +661,10 @@
             dma((8,)),
             dma((2, 4, 2)),
             dma((2, 4, 2)),
-            dma((NZ,)),
+            dma((NZ // 2,)),
             dma((NFLAT,)),
             dma((NFLAT,)),
-            dma((NZ,)),
+            dma((NZ // 2,)),
             dma((NZ,)),
             dma((NZ,)),
             pltpu.SemaphoreType.REGULAR((NZ,)),

time: 89.4 us -> 74.9 us (0.84)
  Pallas kernels: 87.5 us -> 72.3 us
    pallas_call x1, Pallas kernels: 87.5 us -> 72.3 us  [per_device(): pl.pallas_call(kernel, out_shape=jax.ShapeDtypeStruct((ROWS, FEAT), BF16)...]
where the time goes in v3:
time: 74.9 us; the launch traced here: 74 us
  Pallas kernels  72.3 us (97%)
  local copies, waits for them, and re-layouts  1.67 us (2%)
    pallas_call x1, Pallas kernels, per_device(): pl.pallas_call(kernel, out_shape=jax.ShapeDtypeStruct((ROWS, FEAT), BF16)...  72.3 us
    unnamed x1, local copies, waits for them, and re-layouts  1.67 us

profile of v3, /device:TPU:1, one launch (start us, length us, event | category | flops | bytes accessed | tf_op | source)
XLA Modules:
  0.0 74.0 jit_solution(8142632643008792135)
XLA Ops:
  0.0 72.3 %projection.1 = bf16[256,512]{1,0:T(8,128)(2,1)} custom-call(bf16[256,512]{1,0:T(8,128)(2,1)} %act_h.1, bf16[1024,4096]{1,0:T(8,128)(2,1)} %codes_h.1, s32[32,4096]{1,0:T(8,128)} %scl_h.1, f32[256,512]{1,0:T(8,128)} %bitcast.8, f32[1024,128]{1,0:T(8,128)} %bitcast.9, s32[1,256]{1,0:T(1,128)} %bitcast.10, s32[1,192]{1,0:T(1,128)} %bitcast.11), custom_call_target="tpu_custom_call" | custom-call | flops 2147483648 | bytes 11534336 | tf_op jit(solution)/shard_map/projection/pallas_call | solution.py:623
  72.3 1.7 %copy.9 = bf16[256,1,1,512]{3,0,2,1:T(8,128)(2,1)} copy(bf16[256,1,1,512]{3,0,2,1:T(8,128)(2,1)} %bitcast.7) | data formatting | bytes 524288

commit v4 on v3

--- a/solution.py
+++ b/solution.py
@@ -23,7 +23,7 @@
 AD = 4
 SLAB_W = NX * AD * RANK
 
-CHUNKS = ((0, 6), (6, 12))
+CHUNKS = ((0, 1), (2, 3), (4, 5))
 
 
 def kernel(
@@ -107,12 +107,12 @@
         return pltpu.make_async_copy(codes_h.at[:, columns], w_v.at[i], w_sem.at[i])
 
     load_a.start()
+    load_d.start()
+    load_u.start()
     load_w(0).start()
     load_s.start()
-    load_d.start()
     for i in range(1, NROW):
         load_w(i).start()
-    load_u.start()
 
     barrier = pltpu.get_barrier_semaphore()
     for o in range(1, NX):
@@ -184,47 +184,30 @@
         device_id_type=MESH,
     )
 
-    def share(buffer, base, kind):
-        half = AD * RANK // 2
-        where = {
-            "right": (x, pl.ds(0, 2 * half), 1),
-            "left": (x, pl.ds(0, 2 * half), -1),
-            "far_right": ((x + NX - 1) % NX, pl.ds(0, half), 1),
-            "far_left": ((x + 1) % NX, pl.ds(half, half), -1),
-        }
-        at, rows, step = where[kind]
-        n = base + ("right", "left", "far_right", "far_left").index(kind)
-        return pltpu.make_async_remote_copy(
-            src_ref=buffer.at[at, rows],
-            dst_ref=buffer.at[at, rows],
-            send_sem=ad_send.at[n],
-            recv_sem=ad_recv.at[n],
+    def share(buffer, base, step):
+        return pltpu.make_async_remote_copy(
+            src_ref=buffer.at[x],
+            dst_ref=buffer.at[x],
+            send_sem=ad_send.at[base + step],
+            recv_sem=ad_recv.at[base + step],
             device_id=at_x(step),
             device_id_type=MESH,
         )
 
-    def arrived(buffer, base, kind):
-        half = AD * RANK // 2
-        where = {
-            "right": ((x + NX - 1) % NX, pl.ds(0, 2 * half)),
-            "left": ((x + 1) % NX, pl.ds(0, 2 * half)),
-            "far_right": ((x + 2) % NX, pl.ds(0, half)),
-            "far_left": ((x + 2) % NX, pl.ds(half, half)),
-        }
-        at, rows = where[kind]
-        n = base + ("right", "left", "far_right", "far_left").index(kind)
-        return pltpu.make_async_remote_copy(
-            src_ref=buffer.at[at, rows],
-            dst_ref=buffer.at[at, rows],
-            send_sem=ad_send.at[n],
-            recv_sem=ad_recv.at[n],
-            device_id=at_x(1),
-            device_id_type=MESH,
-        )
+    def arrived(buffer, base, step):
+        return pltpu.make_async_remote_copy(
+            src_ref=buffer.at[(x + NX - step) % NX],
+            dst_ref=buffer.at[(x + NX - step) % NX],
+            send_sem=ad_send.at[base + step],
+            recv_sem=ad_recv.at[base + step],
+            device_id=at_x(step),
+            device_id_type=MESH,
+        )
+
     load_d.wait()
     d_all[x] = down_v[...].astype(BF16)
-    share(d_all, 0, "right").start()
-    share(d_all, 0, "left").start()
+    for step in (2, 1, 3):
+        share(d_all, 0, step).start()
     load_a.wait()
     swap_a.start()
 
@@ -322,6 +305,12 @@
             pl.semaphore_wait(hello.at[there], 1)
             send_ids(there).start()
             send_rows(there).start()
+
+    load_u.wait()
+    for q in range(FEAT // 128):
+        u_all[x, :, q * 128 : (q + 1) * 128] = up_v[pl.ds(q, AD * RANK, stride=4), :].astype(BF16)
+    for step in (2, 1, 3):
+        share(u_all, 4, step).start()
 
     half_rows = (pl.ds(0, ROWS // 2), pl.ds(ROWS // 2, ROWS // 2))
 
@@ -372,16 +361,6 @@
     for later in range(NROW + 1, NZ):
         post_later(z + later)
 
-    load_u.wait()
-    for q in range(FEAT // 128):
-        u_all[x, :, q * 128 : (q + 1) * 128] = up_v[pl.ds(q, AD * RANK, stride=4), :].astype(BF16)
-    arrived(d_all, 0, "right").wait_recv()
-    share(d_all, 0, "far_right").start()
-    arrived(d_all, 0, "left").wait_recv()
-    share(d_all, 0, "far_left").start()
-    share(u_all, 4, "right").start()
-    share(u_all, 4, "left").start()
-
     def ring_step(direction, step, half):
         ring(direction, step - 1, half).wait_recv()
         source, landing, _ = ((sp, rp, 1), (sm, rm, -1))[direction]
@@ -436,9 +415,11 @@
             device_id_type=MESH,
         )
 
+    def sources(chunk):
+        return [2 * p + k for p in chunk for k in (0, 1)]
+
     def project(chunk):
-        first, last = chunk
-        for q in range(first, last):
+        for q in sources(chunk):
 
             @pl.when(z != q)
             def _():
@@ -446,19 +427,19 @@
                 take_rows(q).wait_recv()
 
         projected = lax.dot_general(
-            xr[first:last].reshape((last - first) * BLK, FEAT),
+            jnp.concatenate([xr[q] for q in sources(chunk)], axis=0),
             d_all[...].reshape(SLAB_W, FEAT),
             (((1,), (1,)), ((), ())),
             preferred_element_type=F32,
         )
-        for p in range(first // 2, last // 2):
+        for n, p in enumerate(chunk):
             halves = []
-            for q in (2 * p, 2 * p + 1):
-                block = projected[(q - first) * BLK : (q - first + 1) * BLK]
+            for k, q in enumerate((2 * p, 2 * p + 1)):
+                block = projected[(2 * n + k) * BLK : (2 * n + k + 1) * BLK]
                 block = jnp.where(adapter_mask(q), block, 0.0)
                 folded = block[:, 0:128]
-                for k in range(1, SLAB_W // 128):
-                    folded += block[:, k * 128 : (k + 1) * 128]
+                for m in range(1, SLAB_W // 128):
+                    folded += block[:, m * 128 : (m + 1) * 128]
                 folded += pltpu.roll(folded, RANK, 1)
                 halves.append(jnp.where(lane < RANK, folded[: BLK // 2], folded[BLK // 2 :]))
             low_s[p] = jnp.concatenate(halves, axis=0).astype(BF16)
@@ -472,7 +453,7 @@
                 red[flat] = low_s[p]
 
     def reduce_low(chunk):
-        for p in range(chunk[0] // 2, chunk[1] // 2):
+        for p in chunk:
 
             @pl.when(adds_up(p))
             def _():
@@ -492,9 +473,8 @@
                 lax.fori_loop(1, NFLAT, hand_out, 0)
 
     def expand(chunk):
-        first, last = chunk
         spread = []
-        for p in range(first // 2, last // 2):
+        for p in chunk:
 
             @pl.when(jnp.logical_not(adds_up(p)))
             def _():
@@ -518,8 +498,8 @@
             u_all[...].reshape(SLAB_W, FEAT),
             preferred_element_type=F32,
         ).astype(BF16)
-        back_s[first:last] = delta.reshape(last - first, BLK, FEAT)
-        for q in range(first, last):
+        for n, q in enumerate(sources(chunk)):
+            back_s[q] = delta[n * BLK : (n + 1) * BLK]
 
             @pl.when(z != q)
             def _():
@@ -531,28 +511,27 @@
 
     ring_step(0, 1, 0)
     ring_step(1, 1, 1)
-    arrived(d_all, 0, "far_right").wait_recv()
-    arrived(d_all, 0, "far_left").wait_recv()
+    for step in range(1, NX):
+        arrived(d_all, 0, step).wait_recv()
     project(CHUNKS[0])
     ring_step(0, 2, 1)
     ring_step(1, 2, 0)
     ring_step(0, 2, 0)
     ring_step(1, 2, 1)
     reduce_low(CHUNKS[0])
-    arrived(u_all, 4, "right").wait_recv()
-    share(u_all, 4, "far_right").start()
-    arrived(u_all, 4, "left").wait_recv()
-    share(u_all, 4, "far_left").start()
     project(CHUNKS[1])
-    arrived(u_all, 4, "far_right").wait_recv()
-    arrived(u_all, 4, "far_left").wait_recv()
+    for step in range(1, NX):
+        arrived(u_all, 4, step).wait_recv()
     expand(CHUNKS[0])
     reduce_low(CHUNKS[1])
+    project(CHUNKS[2])
+    expand(CHUNKS[1])
+    reduce_low(CHUNKS[2])
     ring_step(0, 3, 1)
     ring_step(1, 3, 0)
     ring_step(0, 3, 0)
     ring_step(1, 3, 1)
-    expand(CHUNKS[1])
+    expand(CHUNKS[2])
 
     for half in (1, 0):
         ring(0, 3, half).wait_recv()
@@ -583,8 +562,8 @@
             send_back(q).wait_send()
 
     for buffer, base in ((d_all, 0), (u_all, 4)):
-        for kind in ("right", "left", "far_right", "far_left"):
-            share(buffer, base, kind).wait_send()
+        for step in range(1, NX):
+            share(buffer, base, step).wait_send()
     for direction in (0, 1):
         ring(direction, 0, direction).wait_send()
         for step in (1, 2, 3):

time: 74.9 us -> 73.6 us (0.983)
  Pallas kernels: 72.3 us -> 71.2 us
    pallas_call x1, Pallas kernels: 72.3 us -> 71.2 us  [per_device(): pl.pallas_call(kernel, out_shape=jax.ShapeDtypeStruct((ROWS, FEAT), BF16)...]
where the time goes in v4:
time: 73.6 us; the launch traced here: 72.9 us
  Pallas kernels  71.2 us (97%)
  local copies, waits for them, and re-layouts  1.67 us (2%)
    pallas_call x1, Pallas kernels, per_device(): pl.pallas_call(kernel, out_shape=jax.ShapeDtypeStruct((ROWS, FEAT), BF16)...  71.2 us
    unnamed x1, local copies, waits for them, and re-layouts  1.67 us

profile of v4, /device:TPU:1, one launch (start us, length us, event | category | flops | bytes accessed | tf_op | source)
XLA Modules:
  0.0 72.9 jit_solution(12106026911491031380)
XLA Ops:
  0.0 71.2 %projection.1 = bf16[256,512]{1,0:T(8,128)(2,1)} custom-call(bf16[256,512]{1,0:T(8,128)(2,1)} %act_h.1, bf16[1024,4096]{1,0:T(8,128)(2,1)} %codes_h.1, s32[32,4096]{1,0:T(8,128)} %scl_h.1, f32[256,512]{1,0:T(8,128)} %bitcast.8, f32[1024,128]{1,0:T(8,128)} %bitcast.9, s32[1,256]{1,0:T(1,128)} %bitcast.10, s32[1,192]{1,0:T(1,128)} %bitcast.11), custom_call_target="tpu_custom_call" | custom-call | flops 2147483648 | bytes 11534336 | tf_op jit(solution)/shard_map/projection/pallas_call | solution.py:602
  71.2 1.7 %copy.9 = bf16[256,1,1,512]{3,0,2,1:T(8,128)(2,1)} copy(bf16[256,1,1,512]{3,0,2,1:T(8,128)(2,1)} %bitcast.7) | data formatting | bytes 524288

commit v5 on v4

--- a/solution.py
+++ b/solution.py
@@ -516,9 +516,9 @@
     project(CHUNKS[0])
     ring_step(0, 2, 1)
     ring_step(1, 2, 0)
+    reduce_low(CHUNKS[0])
     ring_step(0, 2, 0)
     ring_step(1, 2, 1)
-    reduce_low(CHUNKS[0])
     project(CHUNKS[1])
     for step in range(1, NX):
         arrived(u_all, 4, step).wait_recv()

time: 73.6 us -> 74.3 us (level)
  the two profiles are of different devices: /device:TPU:1 before, /device:TPU:704 now
where the time goes in v5:
time: 74.3 us; the launch traced here: 74.1 us
  Pallas kernels  72.5 us (98%)
  local copies, waits for them, and re-layouts  1.67 us (2%)
    pallas_call x1, Pallas kernels, per_device(): pl.pallas_call(kernel, out_shape=jax.ShapeDtypeStruct((ROWS, FEAT), BF16)...  72.5 us
    unnamed x1, local copies, waits for them, and re-layouts  1.67 us

profile of v5, /device:TPU:704, one launch (start us, length us, event | category | flops | bytes accessed | tf_op | source)
XLA Modules:
  0.0 74.1 jit_solution(7684718387318999472)
XLA Ops:
  0.0 72.5 %projection.1 = bf16[256,512]{1,0:T(8,128)(2,1)} custom-call(bf16[256,512]{1,0:T(8,128)(2,1)} %act_h.1, bf16[1024,4096]{1,0:T(8,128)(2,1)} %codes_h.1, s32[32,4096]{1,0:T(8,128)} %scl_h.1, f32[256,512]{1,0:T(8,128)} %bitcast.8, f32[1024,128]{1,0:T(8,128)} %bitcast.9, s32[1,256]{1,0:T(1,128)} %bitcast.10, s32[1,192]{1,0:T(1,128)} %bitcast.11), custom_call_target="tpu_custom_call" | custom-call | flops 2147483648 | bytes 11534336 | tf_op jit(solution)/shard_map/projection/pallas_call | solution.py:602
  72.5 1.7 %copy.9 = bf16[256,1,1,512]{3,0,2,1:T(8,128)(2,1)} copy(bf16[256,1,1,512]{3,0,2,1:T(8,128)(2,1)} %bitcast.7) | data formatting | bytes 524288
